TPU v7x, 512 devices: a whole 4x4x16 slice. The times are simulated.
512 devices in a mesh: gx: 16 (over z), gy: 8 (over y, core), gz: 4 (over x).
Axes of the slice: x: 4, y: 4, z: 16, core: 2. Of those that a mesh axis runs over, the one named last changes fastest.
Arguments:
- positions: float32 [3, 16, 8, 8, 128], P(None, 'gx', 'gy', 'gz'), may hold values from 0 to 16, as said below
- velocity: float32 [3, 16, 8, 8, 128], P(None, 'gx', 'gy', 'gz'), may hold values from -16 to 16
- counts: int32 [16, 8, 8], P('gx', 'gy', 'gz'), may hold values from 0 to 128, as said below
Outputs:
- velocity_new: float32 [3, 16, 8, 8, 128], P(None, 'gx', 'gy', 'gz')
- pressure: float32 [16, 8, 8, 128], P('gx', 'gy', 'gz')
Inputs may be any that keep to these rules, and one draw needn't show every extreme that they name: `positions`: component k of the position of any slot of tile (a, b, c) lies in [t, t + 1), where t is a, b or c for k = 0, 1, 2. A tile's particles fill its first counts[a, b, c] slots. In every column of tiles the bottom tile is full, the tiles below one topmost wet tile hold 96 or more particles, and the tiles above it are empty.
All inputs are finite; a program needn't handle non-finite values.
Results may differ from a plain program's by a relative error of at most 0.0003.
Values sent between devices are 32-bit elements; how exact they have to be, the bound alone decides.
A program may use at most 64 MiB of HBM per device.

v0:
```python
import jax
import jax.numpy as jnp
from jax import lax
from jax.sharding import PartitionSpec as P

P_SIZE = 128
ITERS = 3


DIAG_SHIFT = 0.05
VISCOSITY = 0.5
GRAVITY = 0.1
GRADIENT_GAIN = 32.0


def with_halo(cells, sides, width):
    for axis, dim in sides:
        count = lax.axis_size(axis)
        ends = count - 1
        head = lax.slice_in_dim(cells, 0, width, axis=dim)
        tail = lax.slice_in_dim(cells, cells.shape[dim] - width, cells.shape[dim], axis=dim)
        cells = jnp.concatenate(
            [
                lax.ppermute(tail, axis, [(i, (i + 1) % count) for i in range(ends)]),
                cells,
                lax.ppermute(head, axis, [((i + 1) % count, i) for i in range(ends)]),
            ],
            axis=dim,
        )
    return cells


def tile_pairs(rim_positions, rim_valid, rim_field, fold_step, totals):
    size_x = rim_positions.shape[1] - 2
    size_y = rim_positions.shape[2] - 2
    size_z = rim_positions.shape[3] - 2
    slab_tiles = size_y * size_z
    tile_width = rim_positions.shape[4]

    def near_block(source_array, x_start, y_start, z_start):
        zero_start = jnp.zeros((), jnp.int32)
        window = lax.dynamic_slice(
            source_array,
            (zero_start, x_start, y_start, z_start, zero_start),
            (source_array.shape[0], 1, size_y, size_z, tile_width),
        )
        return window.reshape(source_array.shape[0], slab_tiles, tile_width)

    def slab_totals(x_index):
        unit_step = jnp.ones((), jnp.int32)
        own_positions = near_block(rim_positions, x_index + unit_step, unit_step, unit_step)
        own_valid = near_block(rim_valid, x_index + unit_step, unit_step, unit_step)[0]
        start_totals = jax.tree.map(
            lambda item: jnp.zeros((item.shape[0], slab_tiles, item.shape[2]), jnp.float32), totals
        )

        def one_offset(offset_index, carry):
            offset_code = jnp.asarray(offset_index).astype(jnp.int32)
            step_x = offset_code // 9
            step_y = offset_code // 3 % 3
            step_z = offset_code % 3
            near_positions = near_block(rim_positions, x_index + step_x, step_y, step_z)
            near_valid = near_block(rim_valid, x_index + step_x, step_y, step_z)[0]
            near_field = near_block(rim_field, x_index + step_x, step_y, step_z)
            offset = own_positions[:, :, :, None] - near_positions[:, :, None, :]
            distance = offset[0] * offset[0] + offset[1] * offset[1] + offset[2] * offset[2]
            closeness = jnp.maximum(1.0 - distance, 0.0)
            weight = closeness * closeness * own_valid[:, :, None] * near_valid[:, None, :]
            return fold_step(carry, weight, offset, near_field)

        return lax.fori_loop(0, 27, one_offset, start_totals)

    stacked = lax.map(slab_totals, jnp.arange(size_x, dtype=jnp.int32))
    return jax.tree.map(
        lambda block_out: jnp.moveaxis(block_out, 0, 1).reshape(
            block_out.shape[1], size_x * slab_tiles, block_out.shape[3]
        ),
        stacked,
    )


def flat_zeros(rim_positions, components):
    tile_count = (
        (rim_positions.shape[1] - 2) * (rim_positions.shape[2] - 2) * (rim_positions.shape[3] - 2)
    )
    return jnp.zeros((components, tile_count, rim_positions.shape[4]), jnp.float32)


def unflat(flat_values, rim_positions):
    return flat_values.reshape(
        flat_values.shape[0],
        rim_positions.shape[1] - 2,
        rim_positions.shape[2] - 2,
        rim_positions.shape[3] - 2,
        flat_values.shape[2],
    )


def viscous_fold(totals, weight, offset, near_field):
    near_sums, row_sums = totals
    near_sums = near_sums + jnp.einsum(
        "tij,ctj->cti", weight, near_field, precision=lax.Precision.HIGHEST
    )
    return (near_sums, row_sums + jnp.sum(weight, axis=2)[None])


def divergence_fold(totals, weight, offset, near_field):
    lever_sums, flux_sums = totals
    levered = weight[None] * offset
    flux_sums = (
        flux_sums
        + jnp.einsum("ctij,ctj->ti", levered, near_field, precision=lax.Precision.HIGHEST)[None]
    )
    return (lever_sums + jnp.sum(levered, axis=3), flux_sums)


def laplace_fold(totals, weight, offset, near_field):
    return totals + jnp.einsum("tij,ctj->cti", weight, near_field, precision=lax.Precision.HIGHEST)


def gradient_fold(totals, weight, offset, near_field):
    levered = weight[None] * offset
    return totals + jnp.einsum(
        "ctij,tj->cti", levered, near_field[0], precision=lax.Precision.HIGHEST
    )


def viscous_pass(rim_positions, rim_valid, rim_field):
    near_sums, row_sums = tile_pairs(
        rim_positions,
        rim_valid,
        rim_field,
        viscous_fold,
        (flat_zeros(rim_positions, 3), flat_zeros(rim_positions, 1)),
    )
    return (unflat(near_sums, rim_positions), unflat(row_sums, rim_positions))


def divergence_pass(rim_positions, rim_valid, rim_field):
    lever_sums, flux_sums = tile_pairs(
        rim_positions,
        rim_valid,
        rim_field,
        divergence_fold,
        (flat_zeros(rim_positions, 3), flat_zeros(rim_positions, 1)),
    )
    return (unflat(lever_sums, rim_positions), unflat(flux_sums, rim_positions))


def laplace_pass(rim_positions, rim_valid, rim_field):
    return unflat(
        tile_pairs(rim_positions, rim_valid, rim_field, laplace_fold, flat_zeros(rim_positions, 1)),
        rim_positions,
    )


def gradient_pass(rim_positions, rim_valid, rim_field):
    return unflat(
        tile_pairs(
            rim_positions, rim_valid, rim_field, gradient_fold, flat_zeros(rim_positions, 3)
        ),
        rim_positions,
    )


def advance(velocity, valid_mask, near_sums, row_sums):
    gravity_pull = jnp.array([0.0, 0.0, -GRAVITY], jnp.float32).reshape(3, 1, 1, 1, 1)
    return valid_mask * (
        velocity + VISCOSITY / P_SIZE * (near_sums - row_sums * velocity) + gravity_pull
    )


def operate(direction, rim_positions, rim_valid, diagonal):
    rim_direction = with_halo(direction, (("gx", 1), ("gy", 2), ("gz", 3)), 1)
    return (
        rim_direction,
        diagonal * direction - laplace_pass(rim_positions, rim_valid, rim_direction) / P_SIZE,
    )


def norm_sum(residual, precond):
    return lax.psum(jnp.sum(residual * precond), ("gx", "gy", "gz"))


def on_device(positions, velocity, counts):
    slot_ids = jnp.arange(positions.shape[4], dtype=jnp.int32)
    valid_mask = (slot_ids[None, None, None, :] < counts[:, :, :, None]).astype(jnp.float32)[None]
    rim_positions, rim_valid, rim_velocity = (
        with_halo(positions, (("gx", 1), ("gy", 2), ("gz", 3)), 1),
        with_halo(valid_mask, (("gx", 1), ("gy", 2), ("gz", 3)), 1),
        with_halo(velocity, (("gx", 1), ("gy", 2), ("gz", 3)), 1),
    )
    near_sums, row_sums = viscous_pass(rim_positions, rim_valid, rim_velocity)
    predicted = advance(velocity, valid_mask, near_sums, row_sums)
    rim_predicted = with_halo(predicted, (("gx", 1), ("gy", 2), ("gz", 3)), 1)
    diagonal = DIAG_SHIFT + row_sums / P_SIZE
    lever_sums, flux_sums = divergence_pass(rim_positions, rim_valid, rim_predicted)
    source = -(GRADIENT_GAIN / P_SIZE) * (
        jnp.sum(predicted * lever_sums, axis=0, keepdims=True) - flux_sums
    )
    pressure = jnp.zeros_like(source)
    residual = source
    precond = residual / diagonal
    direction = precond
    norm_now = norm_sum(residual, precond)
    for iteration in range(ITERS):
        rim_direction, applied = operate(direction, rim_positions, rim_valid, diagonal)
        step_size = norm_now / lax.psum(jnp.sum(direction * applied), ("gx", "gy", "gz"))
        pressure = pressure + step_size * direction
        residual = residual - step_size * applied
        if iteration + 1 < ITERS:
            precond = residual / diagonal
            norm_next = norm_sum(residual, precond)
            direction = precond + norm_next / norm_now * direction
            norm_now = norm_next
    rim_pressure = with_halo(pressure, (("gx", 1), ("gy", 2), ("gz", 3)), 1)
    moments = gradient_pass(rim_positions, rim_valid, rim_pressure)
    velocity_new = predicted - GRADIENT_GAIN / P_SIZE * (pressure * lever_sums - moments)
    return (velocity_new, pressure[0])


def solution(mesh):
    in_specs = (
        P(None, "gx", "gy", "gz", None),
        P(None, "gx", "gy", "gz", None),
        P("gx", "gy", "gz"),
    )
    out_specs = (P(None, "gx", "gy", "gz", None), P("gx", "gy", "gz", None))
    return jax.shard_map(
        on_device, mesh=mesh, in_specs=in_specs, out_specs=out_specs, check_vma=False
    )
```

profile of v0, /device:TPU:1, one launch (start us, length us, event | category | flops | bytes accessed | tf_op | source)
XLA Modules:
  0.0 858.0 jit_solution(1430521027441401658)
XLA Ops:
  1.4 4.5 collective-permute-start.12
  7.2 4.2 collective-permute-start
  12.7 4.2 collective-permute-start.6
  18.2 4.8 collective-permute-start.14
  44.1 4.3 collective-permute-start.10
  58.3 24.4 %while.152 = (s32[]{:T(128)}, f32[3,2,128]{2,0,1:T(4,128)S(1)}, f32[1,2,128]{2,1,0:T(2,128)S(1)}, f32[3,3,3,4,128]{4,0,3,2,1:T(4,128)S(1)}, f32[3,1,1,2,128]{4,3...) while((s32[]{:T(128)}, f32[3,2,128]{2,0,1:T(4,128)S(1)}, ...), condition=%wide.region_2.3_spmd.clone, body=%wide.region_0.2_spmd.clone.sunk | while | flops 1640740 | bytes 1081868 | solution.py:71
  83.4 5.2 collective-permute-start.18
  89.9 4.5 collective-permute-done.19
  94.5 5.1 collective-permute-start.20
  112.2 40.3 %while.153 = (s32[]{:T(128)}, f32[3,2,128]{2,1,0:T(2,128)S(1)}, f32[1,2,128]{2,1,0:T(2,128)S(1)}, f32[3,1,1,2,128]{4,3,0,2,1:T(2,128)S(1)}, f32[3,3,3,4,128]{4,3...) while((s32[]{:T(128)}, f32[3,2,128]{2,1,0:T(2,128)S(1)}, ...), condition=%wide.region_5.6_spmd.clone, body=%wide.region_3.5_spmd.clone.sunk | while | flops 2098980 | bytes 1235468 | solution.py:71
  152.5 4.8 collective-permute-start.24
  158.7 4.8 collective-permute-done.25
  163.5 4.2 collective-permute-start.26
  179.9 21.0 %while.154 = (s32[]{:T(128)}, f32[1,2,128]{2,1,0:T(2,128)S(1)}, f32[1,3,3,4,128]{4,3,2,1,0:T(4,128)S(1)}, f32[3,1,1,2,128]{4,3,2,1,0:T(2,128)S(1)}, f32[3,3,3,4,...) while((s32[]{:T(128)}, f32[1,2,128]{2,1,0:T(2,128)S(1)}, ...), condition=%wide.region_10.11_spmd.clone, body=%wide.region_9.10_spmd.clone.sunk | while | flops 820260 | bytes 811523 | solution.py:71
  201.5 106.7 %all-reduce = (f32[]{:T(128)}, f32[]{:T(128)}) all-reduce(f32[]{:T(128)} %get-tuple-element.1779, f32[]{:T(128)} %get-tuple-element.1778), channel_id=1, replica_groups=mesh['gx'=16,'gy'=8,'gz'=4] {'gx','gy','gz'}, use_global_device_ids=true, to_apply=%region_8.9 | all-reduce | flops 2 | bytes 16 | tf_op jit(solution)/shard_map/psum | solution.py:182
  310.1 98.5 %psum.44 = f32[]{:T(128)} all-reduce(f32[]{:T(128)} %get-tuple-element.1874), channel_id=1, replica_groups=mesh['gx'=16,'gy'=8,'gz'=4] {'gx','gy','gz'}, use_global_device_ids=true, to_apply=%region_14.15 | all-reduce | flops 1 | bytes 8 | tf_op jit(solution)/shard_map/psum | solution.py:182
  418.0 4.3 collective-permute-start.32
  433.2 21.0 %while.155 = (s32[]{:T(128)}, f32[1,2,128]{2,1,0:T(2,128)S(1)}, f32[1,3,3,4,128]{4,3,2,1,0:T(4,128)S(1)}, f32[3,1,1,2,128]{4,3,2,1,0:T(2,128)S(1)}, f32[3,3,3,4,...) while((s32[]{:T(128)}, f32[1,2,128]{2,1,0:T(2,128)S(1)}, ...), condition=%wide.region_16.17_spmd.clone, body=%wide.region_15.16_spmd.clone.sunk | while | flops 820260 | bytes 811523 | solution.py:71
  454.8 100.8 %psum.45 = f32[]{:T(128)} all-reduce(f32[]{:T(128)} %get-tuple-element.1872), channel_id=1, replica_groups=mesh['gx'=16,'gy'=8,'gz'=4] {'gx','gy','gz'}, use_global_device_ids=true, to_apply=%region_18.19 | all-reduce | flops 1 | bytes 8 | tf_op jit(solution)/shard_map/psum | solution.py:208
  557.6 98.6 %psum.46 = f32[]{:T(128)} all-reduce(f32[]{:T(128)} %multiply_reduce_fusion.1), channel_id=1, replica_groups=mesh['gx'=16,'gy'=8,'gz'=4] {'gx','gy','gz'}, use_global_device_ids=true, to_apply=%region_20.21 | all-reduce | flops 1 | bytes 8 | tf_op jit(solution)/shard_map/psum | solution.py:182
  665.6 4.2 collective-permute-start.38
  680.8 21.0 %while.156 = (s32[]{:T(128)}, f32[1,2,128]{2,1,0:T(2,128)S(1)}, f32[1,3,3,4,128]{4,3,2,1,0:T(4,128)S(1)}, f32[3,1,1,2,128]{4,3,2,1,0:T(2,128)S(1)}, f32[3,3,3,4,...) while((s32[]{:T(128)}, f32[1,2,128]{2,1,0:T(2,128)S(1)}, ...), condition=%wide.region_22.23_spmd.clone, body=%wide.region_21.22_spmd.clone.sunk | while | flops 820260 | bytes 811523 | solution.py:71
  702.4 100.9 %psum.47 = f32[]{:T(128)} all-reduce(f32[]{:T(128)} %fusion.115), channel_id=1, replica_groups=mesh['gx'=16,'gy'=8,'gz'=4] {'gx','gy','gz'}, use_global_device_ids=true, to_apply=%region_24.25 | all-reduce | flops 1 | bytes 8 | tf_op jit(solution)/shard_map/psum | solution.py:208
  826.4 31.0 %while.157 = (s32[]{:T(128)}, f32[3,2,128]{2,1,0:T(2,128)S(1)}, f32[1,3,3,4,128]{4,3,2,1,0:T(4,128)S(1)}, f32[3,1,1,2,128]{4,3,2,1,0:T(2,128)S(1)}, f32[3,3,3,4,...) while((s32[]{:T(128)}, f32[3,2,128]{2,1,0:T(2,128)S(1)}, ...), condition=%wide.region_26.27_spmd.clone, body=%wide.region_25.26_spmd.clone.sunk | while | flops 1804324 | bytes 1088003 | solution.py:71
  (1395 shorter events, 265.4 us)
Async XLA Ops:
  1.4 15.6 %collective-permute-start.12 = (f32[1,1,1,2,128]{4,3,2,1,0:T(2,128)S(1)}, f32[1,1,1,2,128]{4,3,2,1,0:T(2,128)S(1)}, u32[]{:S(2)}, u32[]{:S(2)}) collective-permute-start(f32[1,1,1,2,128]{4,3,2,1,0:T(2,128)S(1)} %compare_convert_fusion.6), channel_id=1, source_target_pairs={{0,32},{32,64},{64,96},{96,128},{128,160},{160,192},{192,224},{224... | collective-permute-start | bytes 3080 | tf_op jit(solution)/shard_map/ppermute | solution.py:24
  5.9 12.4 %collective-permute-start.13 = (f32[1,1,1,2,128]{4,3,2,1,0:T(2,128)S(1)}, f32[1,1,1,2,128]{4,3,2,1,0:T(2,128)S(1)}, u32[]{:S(2)}, u32[]{:S(2)}) collective-permute-start(f32[1,1,1,2,128]{4,3,2,1,0:T(2,128)S(1)} %compare_convert_fusion.6), channel_id=1, source_target_pairs={{32,0},{64,32},{96,64},{128,96},{160,128},{192,160},{224,192},{256... | collective-permute-start | bytes 3080 | tf_op jit(solution)/shard_map/ppermute | solution.py:26
  7.2 15.9 %collective-permute-start = (f32[3,1,1,2,128]{4,0,3,2,1:T(4,128)S(1)}, f32[3,1,1,2,128]{4,0,3,2,1:T(4,128)S(1)}, u32[]{:S(2)}, u32[]{:S(2)}) collective-permute-start(f32[3,1,1,2,128]{4,0,3,2,1:T(4,128)S(1)} %copy.12), channel_id=1, source_target_pairs={{0,32},{32,64},{64,96},{96,128},{128,160},{160,192},{192,224},{224... | collective-permute-start | bytes 9224 | tf_op jit(solution)/shard_map/ppermute | solution.py:24
  11.4 14.7 %collective-permute-start.1 = (f32[3,1,1,2,128]{4,0,3,2,1:T(4,128)S(1)}, f32[3,1,1,2,128]{4,0,3,2,1:T(4,128)S(1)}, u32[]{:S(2)}, u32[]{:S(2)}) collective-permute-start(f32[3,1,1,2,128]{4,0,3,2,1:T(4,128)S(1)} %copy.12), channel_id=1, source_target_pairs={{32,0},{64,32},{96,64},{128,96},{160,128},{192,160},{224,192},{256... | collective-permute-start | bytes 9224 | tf_op jit(solution)/shard_map/ppermute | solution.py:26
  12.7 16.0 %collective-permute-start.6 = (f32[3,1,1,2,128]{4,3,2,1,0:T(2,128)S(1)}, f32[3,1,1,2,128]{4,3,2,1,0:T(2,128)S(1)}, u32[]{:S(2)}, u32[]{:S(2)}) collective-permute-start(f32[3,1,1,2,128]{4,3,2,1,0:T(2,128)S(1)} %copy-done), channel_id=1, source_target_pairs={{0,32},{32,64},{64,96},{96,128},{128,160},{160,192},{192,224},{224... | collective-permute-start | bytes 9224 | tf_op jit(solution)/shard_map/ppermute | solution.py:24
  16.9 18.2 %collective-permute-start.7 = (f32[3,1,1,2,128]{4,3,2,1,0:T(2,128)S(1)}, f32[3,1,1,2,128]{4,3,2,1,0:T(2,128)S(1)}, u32[]{:S(2)}, u32[]{:S(2)}) collective-permute-start(f32[3,1,1,2,128]{4,3,2,1,0:T(2,128)S(1)} %copy-done), channel_id=1, source_target_pairs={{32,0},{64,32},{96,64},{128,96},{160,128},{192,160},{224,192},{256... | collective-permute-start | bytes 9224 | tf_op jit(solution)/shard_map/ppermute | solution.py:26
  18.2 12.4 %collective-permute-start.14 = (f32[1,3,1,2,128]{4,3,2,1,0:T(2,128)S(1)}, f32[1,3,1,2,128]{4,3,2,1,0:T(2,128)S(1)}, u32[]{:S(2)}, u32[]{:S(2)}) collective-permute-start(f32[1,3,1,2,128]{4,3,2,1,0:T(2,128)S(1)} %pad_maximum_fusion.17), channel_id=1, source_target_pairs={{0,4},{4,8},{8,12},{12,16},{16,20},{20,24},{24,28},{1,5},{5,9},{9,... | collective-permute-start | bytes 9224 | tf_op jit(solution)/shard_map/ppermute | solution.py:24
  23.1 7.6 collective-permute-start.15
  26.1 23.6 %collective-permute-start.2 = (f32[3,3,1,2,128]{4,0,3,2,1:T(4,128)S(1)}, f32[3,3,1,2,128]{4,0,3,2,1:T(4,128)S(1)}, u32[]{:S(2)}, u32[]{:S(2)}) collective-permute-start(f32[3,3,1,2,128]{4,0,3,2,1:T(4,128)S(1)} %constant_dynamic-update-slice_fusion), channel_id=1, source_target_pairs={{0,4},{4,8},{8,12},{12,16},{16,20},{20,24},{24,28},{1,5},{5,9},{9,... | collective-permute-start | bytes 27656 | tf_op jit(solution)/shard_map/ppermute | solution.py:24
  28.7 21.0 %collective-permute-start.3 = (f32[3,3,1,2,128]{4,0,3,2,1:T(4,128)S(1)}, f32[3,3,1,2,128]{4,0,3,2,1:T(4,128)S(1)}, u32[]{:S(2)}, u32[]{:S(2)}) collective-permute-start(f32[3,3,1,2,128]{4,0,3,2,1:T(4,128)S(1)} %constant_dynamic-update-slice_fusion), channel_id=1, source_target_pairs={{4,0},{8,4},{12,8},{16,12},{20,16},{24,20},{28,24},{5,1},{9,5},{13... | collective-permute-start | bytes 27656 | tf_op jit(solution)/shard_map/ppermute | solution.py:26
  30.7 8.4 collective-permute-start.16
  33.8 7.2 collective-permute-start.17
  35.1 5.9 collective-permute-start.8
  44.1 10.9 %collective-permute-start.10 = (f32[3,3,3,1,128]{4,3,2,1,0:T(1,128)S(1)}, f32[3,3,3,1,128]{4,3,2,1,0:T(1,128)S(1)}, u32[]{:S(2)}, u32[]{:S(2)}) collective-permute-start(f32[3,3,3,1,128]{4,3,2,1,0:T(1,128)S(1)} %get-tuple-element.1882), channel_id=1, source_target_pairs={{0,1},{1,2},{2,3},{4,5},{5,6},{6,7},{8,9},{9,10},{10,11},{12,13},{... | collective-permute-start | bytes 41480 | tf_op jit(solution)/shard_map/ppermute | solution.py:24
  48.4 6.7 collective-permute-start.11
  83.4 6.5 collective-permute-start.18
  88.6 5.8 collective-permute-start.19
  94.5 7.0 collective-permute-start.20
  152.5 6.2 collective-permute-start.24
  157.4 6.1 collective-permute-start.25
  163.5 6.2 collective-permute-start.26
  418.0 6.2 collective-permute-start.32
  665.6 6.1 collective-permute-start.38
  811.4 6.2 collective-permute-start.44
  (28 other events, 125.3 us)
where the time goes:
time: 860 us; the launch traced here: 858 us
  blocking collectives  506 us (59%)
  starting transfers between devices  125 us (15%)
  matrix products  72 us (8%)
  other arithmetic  64.9 us (8%)
  waiting for transfers between devices  54.6 us (6%)
  loops' own time  19.8 us (2%)
    psum x3, blocking collectives, norm_sum(): return lax.psum(jnp.sum(residual * precond), ('gx', 'gy', 'gz'))  304 us
    psum x2, blocking collectives, on_device(): lax.psum(jnp.sum(direction * applied), ('gx', 'gy', 'gz'))  202 us
    ppermute x24, starting transfers between devices, with_halo(): lax.ppermute(tail, axis, [(i, (i + 1) % count) for i in range(ends)])  87.5 us
    ppermute x24, waiting for transfers between devices, with_halo(): lax.ppermute(head, axis, [((i + 1) % count, i) for i in range(ends)])  54.5 us
    ppermute x24, starting transfers between devices, with_halo(): lax.ppermute(head, axis, [((i + 1) % count, i) for i in range(ends)])  37.2 us
    dot_general x81, matrix products, laplace_fold(): jnp.einsum('tij,ctj->cti', weight, near_field, precision=lax.Precision.HI...  30.4 us
    sub x162, other arithmetic, one_offset(): offset = own_positions[:, :, :, None] - near_positions[:, :, None, :]  26.4 us
    another operation x6, loops' own time, slab_totals(): return lax.fori_loop(0, 27, one_offset, start_totals)  19.8 us
  transfers between devices with their start and end apart: 48, of which 17 were waited for; matrix products, arithmetic and copies ran while one was open for 0% of the time, Pallas kernels for 0%

commit v1 on v0

v1 whole, which is shorter than its diff:
```python
import functools
import itertools

import jax
import jax.numpy as jnp
from jax import lax
from jax.experimental import pallas as pl
from jax.experimental.pallas import tpu as pltpu
from jax.sharding import PartitionSpec as P

P_SIZE = 128
DIAG_SHIFT = 0.05
VISCOSITY = 0.5
GRAVITY = 0.1
GRADIENT_GAIN = 32.0

MESH = pl.DeviceIdType.MESH
F32 = jnp.float32
AXES = ("gx", "gy", "gz")
OFFSETS = sorted((o for o in itertools.product((-1, 0, 1), repeat=3) if any(o)), key=lambda o: -sum(map(abs, o)))
N_OFF = len(OFFSETS)
OWN = 17
GROUPS = (
    ((0, 0),),
    ((-1, 0), (1, 0), (0, -1), (0, 1)),
    ((-1, -1), (-1, 1), (1, -1), (1, 1)),
)


def near_index(column, step_z):
    return ((column[0] + 1) * 3 + column[1] + 1) * 3 + step_z


def tile_index(column, own, step_z):
    return ((column[0] + 1) * 3 + column[1] + 1) * 4 + own + step_z


ALL_COLUMNS = tuple(c for g in GROUPS for c in g)


def kernel(sizes, pos, vel, counts, vel_out, pres_out, x_own, x_halo, x_col, weights, sums, cols, p_own, p_halo, t_own,
           t_halo, levered, a_own, a_halo, b_own, b_halo, send, recv, a_sem, b_sem):
    me = [lax.axis_index(axis) for axis in AXES]

    def device(offset):
        return tuple(lax.rem(m + (d + n), n) for m, d, n in zip(me, offset, sizes))

    plane = [(0, a, b) for a in range(sizes[1]) for b in range(sizes[2]) if a or b]
    length = [(a, 0, 0) for a in range(1, sizes[0])]
    inside = {
        (1, -1): me[1] > 0, (1, 1): me[1] < sizes[1] - 1,
        (2, -1): me[2] > 0, (2, 1): me[2] < sizes[2] - 1,
    }

    def exists(dy, dz):
        terms = [inside[axis, d] for axis, d in ((1, dy), (2, dz)) if d]
        if not terms:
            return None
        return terms[0] if len(terms) == 1 else jnp.logical_and(*terms)

    def under(condition, body):
        if condition is None:
            body()
        else:
            pl.when(condition)(body)

    x_halo[...] = jnp.zeros_like(x_halo)
    p_halo[...] = jnp.zeros_like(p_halo)
    t_halo[...] = jnp.zeros_like(t_halo)

    barrier = pltpu.get_barrier_semaphore()
    greeted = OFFSETS + [(3, 0, 0), (-3, 0, 0)]
    for offset in greeted:
        pl.semaphore_signal(barrier, inc=1, device_id=device(offset), device_id_type=MESH)

    lanes = lax.broadcasted_iota(jnp.int32, (1, P_SIZE), 1)
    valid = [(lanes < counts[t]).astype(F32) for t in range(2)]
    for t in range(2):
        for k in range(3):
            x_own[t, k : k + 1] = pos[k, t : t + 1]
            x_own[t, 3 + k : 4 + k] = vel[k, t : t + 1]
        x_own[t, 6:7] = valid[t]
        x_own[t, 7:8] = jnp.zeros((1, P_SIZE), F32)
        x_halo[OWN + t] = x_own[t]
        for k in range(3):
            x_col[t, k] = jnp.broadcast_to(pos[k, t : t + 1], (P_SIZE, P_SIZE)).T
    pl.semaphore_wait(barrier, len(greeted))

    def copy(phase, own, halo, offset):
        dx, dy, dz = offset
        place = ((1 - dx) * 3 + 1 - dy) * 4
        if dz == 0:
            source, target = own, halo.at[place + 1 : place + 3]
        elif dz > 0:
            source, target = own.at[1:2], halo.at[place : place + 1]
        else:
            source, target = own.at[0:1], halo.at[place + 3 : place + 4]
        i = OFFSETS.index(offset)
        return pltpu.make_async_remote_copy(
            source, target, send.at[phase, i], recv.at[phase, i], device_id=device(offset), device_id_type=MESH
        )

    combos = sorted(itertools.product((-1, 0, 1), repeat=2), key=lambda c: -sum(map(abs, c)))

    def start(phase, own, halo):
        for dy, dz in combos:
            def body(dy=dy, dz=dz):
                for dx in (-1, 1, 0):
                    if dx or dy or dz:
                        copy(phase, own, halo, (dx, dy, dz)).start()
            under(exists(dy, dz), body)

    def arrive(phase, own, halo, columns):
        for dy, dz in combos[::-1]:
            steps = [-c[0] for c in columns if c[1] == -dy and (c[0] or dy or dz)]
            if steps:
                def body(dy=dy, dz=dz, steps=steps):
                    for dx in steps:
                        copy(phase, own, halo, (dx, dy, dz)).wait_recv()
                under(exists(-dy, -dz), body)

    def sent(phase, own, halo):
        for dy, dz in combos:
            def body(dy=dy, dz=dz):
                for dx in (-1, 1, 0):
                    if dx or dy or dz:
                        copy(phase, own, halo, (dx, dy, dz)).wait_send()
            under(exists(dy, dz), body)

    def to_rows(n):
        for r in range(0, P_SIZE, 16):
            block = jnp.zeros((16, P_SIZE), F32)
            for a in range(2):
                for q in range(n):
                    total = jnp.sum(sums[a, q, r : r + 16], axis=1, keepdims=True)
                    block = jnp.where(lanes == 16 * a + q, total, block)
            cols[r : r + 16] = block
        turned = cols[...].T
        return [[turned[16 * a + q : 16 * a + q + 1] for q in range(n)] for a in range(2)]

    def apply(n, row_of, depth):
        @pl.loop(0, P_SIZE // depth)
        def _(block):
            at = pl.ds(pl.multiple_of(block * depth, depth), depth)
            for a in range(2):
                totals = [jnp.zeros((depth, P_SIZE), F32)] * n
                for column in ALL_COLUMNS:
                    for dz in range(3):
                        tile = tile_index(column, a, dz)
                        w = weights[a, near_index(column, dz), at]
                        for q in range(n):
                            totals[q] = totals[q] + w * row_of(tile, q)
                for q in range(n):
                    sums[a, q, at] = totals[q]
        return to_rows(n)

    start(0, x_own, x_halo)
    for number, columns in enumerate(GROUPS):
        arrive(0, x_own, x_halo, columns)

        @pl.loop(0, P_SIZE // 16)
        def _(block, number=number, columns=columns):
            at = pl.ds(pl.multiple_of(block * 16, 16), 16)
            for a in range(2):
                mine = [x_col[a, k, at] for k in range(3)]
                if number:
                    totals = [sums[a, q, at] for q in range(7)]
                else:
                    totals = [jnp.zeros((16, P_SIZE), F32)] * 7
                for column in columns:
                    for dz in range(3):
                        tile = tile_index(column, a, dz)
                        d = [mine[k] - x_halo[tile, k : k + 1] for k in range(3)]
                        near = jnp.maximum(1.0 - (d[0] * d[0] + d[1] * d[1] + d[2] * d[2]), 0.0)
                        w = near * near * x_halo[tile, 6:7]
                        weights[a, near_index(column, dz), at] = w
                        totals[0] = totals[0] + w
                        for k in range(3):
                            totals[1 + k] = totals[1 + k] + w * x_halo[tile, 3 + k : 4 + k]
                            totals[4 + k] = totals[4 + k] + w * d[k]
                for q in range(7):
                    sums[a, q, at] = totals[q]

    rows = to_rows(7)
    scale = 1.0 / P_SIZE
    centre = [s * 0.5 for s in (sizes[0], sizes[1], sizes[2] * 2)]
    diagonal, lever, predicted, x = [], [], [], []
    for a in range(2):
        row = rows[a][0] * valid[a]
        v = [vel[k, a : a + 1] for k in range(3)]
        x.append([pos[k, a : a + 1] - centre[k] for k in range(3)])
        diagonal.append(DIAG_SHIFT + row * scale)
        lever.append([rows[a][4 + k] * valid[a] for k in range(3)])
        p = [valid[a] * (v[k] + VISCOSITY * scale * (rows[a][1 + k] - row * v[k]) - (GRAVITY if k == 2 else 0.0)) for k in range(3)]
        predicted.append(p)
        for k in range(3):
            p_own[a, k : k + 1] = p[k]
        p_own[a, 3:4] = p[0] * x[a][0] + p[1] * x[a][1] + p[2] * x[a][2]
    start(1, p_own, p_halo)
    p_halo[OWN : OWN + 2] = p_own[...]
    arrive(1, p_own, p_halo, ALL_COLUMNS)
    rows = apply(4, lambda tile, q: p_halo[tile, q : q + 1], 16)
    basis, source = [[], [], [], []], []
    for a in range(2):
        flux = x[a][0] * rows[a][0] + x[a][1] * rows[a][1] + x[a][2] * rows[a][2] - rows[a][3]
        dot = predicted[a][0] * lever[a][0] + predicted[a][1] * lever[a][1] + predicted[a][2] * lever[a][2]
        source.append(valid[a] * (-(GRADIENT_GAIN * scale) * (dot - flux)))
        basis[0].append(source[a] / diagonal[a])
        t_own[0, a] = basis[0][a]
    inverse = [scale * valid[a] / diagonal[a] for a in range(2)]

    spread = []
    for k in range(3):
        start(2 + k, t_own.at[k], t_halo.at[k])
        t_halo[k, OWN : OWN + 2] = t_own[k]
        arrive(2 + k, t_own.at[k], t_halo.at[k], ALL_COLUMNS)
        rows = apply(1, lambda tile, q, k=k: t_halo[k, tile], 32)
        spread.append([rows[a][0] for a in range(2)])
        for a in range(2):
            basis[k + 1].append(spread[k][a] * inverse[a])
            if k < 2:
                t_own[k + 1, a] = basis[k + 1][a]

    packed = jnp.zeros((1, P_SIZE), F32)
    for q in range(6):
        i, j = q // 2, (q + 1) // 2
        terms = sum(diagonal[a] * basis[i][a] * basis[j][a] for a in range(2))
        packed = jnp.where(lanes == q, jnp.sum(terms, axis=1, keepdims=True), packed)

    def share(peers, own, halo, sem):
        for i, offset in enumerate(peers):
            pltpu.make_async_remote_copy(
                own, halo.at[i : i + 1], sem.at[0], sem.at[1], device_id=device(offset), device_id_type=MESH
            ).start()

    def gathered(peers, own, halo, sem):
        pltpu.make_async_copy(halo, halo, sem.at[1]).wait()
        return own[0] + jnp.sum(halo[...], axis=0)

    a_own[0] = packed
    share(plane, a_own, a_halo, a_sem)

    for tile in range(36):
        local = x_halo[tile]
        for c in range(3):
            levered[c, tile] = (local[c : c + 1] - centre[c]) * jnp.concatenate([t_halo[k, tile] for k in range(3)] + [jnp.zeros((5, P_SIZE), F32)], axis=0)
    rows = apply(9, lambda tile, q: levered[q // 3, tile, q % 3 : q % 3 + 1], 16)
    moved = []
    for a in range(2):
        moved.append([
            [basis[k][a] * lever[a][c] - valid[a] * (x[a][c] * spread[k][a] - rows[a][3 * c + k]) for k in range(3)]
            for c in range(3)
        ])

    b_own[0] = gathered(plane, a_own, a_halo, a_sem)
    share(length, b_own, b_halo, b_sem)
    sent(0, x_own, x_halo)
    sent(1, p_own, p_halo)
    for k in range(3):
        sent(2 + k, t_own.at[k], t_halo.at[k])
    pltpu.make_async_copy(a_halo, a_halo, a_sem.at[0]).wait()
    total = gathered(length, b_own, b_halo, b_sem)

    m = [jnp.sum(jnp.where(lanes == q, total, 0.0), axis=1, keepdims=True) for q in range(6)]
    g00, g01, g11, g12, g22 = (m[q] - m[q + 1] for q in range(5))
    l1, l2 = g01 / g00, g11 / g00
    a11, a12, a22 = g11 - l1 * g01, g12 - l1 * g11, g22 - l2 * g11
    y1, y2 = m[1] - l1 * m[0], m[2] - l2 * m[0]
    l3 = a12 / a11
    c2 = (y2 - l3 * y1) / (a22 - l3 * a12)
    c1 = (y1 - a12 * c2) / a11
    c0 = (m[0] - g01 * c1 - g11 * c2) / g00
    weight = [c0, c1, c2]
    for a in range(2):
        pres_out[a : a + 1] = sum(weight[k] * basis[k][a] for k in range(3))
        for c in range(3):
            vel_out[c, a : a + 1] = predicted[a][c] - (GRADIENT_GAIN * scale) * sum(weight[k] * moved[a][c][k] for k in range(3))
    pltpu.make_async_copy(b_halo, b_halo, b_sem.at[0]).wait()


def solution(mesh):
    sizes = tuple(mesh.shape[axis] for axis in AXES)

    def on_device(positions, velocity, counts):
        vmem = pl.BlockSpec(memory_space=pltpu.VMEM)
        n_plane, n_length = sizes[1] * sizes[2] - 1, sizes[0] - 1
        moved, pressure = pl.pallas_call(
            functools.partial(kernel, sizes),
            out_shape=(jax.ShapeDtypeStruct((3, 2, P_SIZE), F32), jax.ShapeDtypeStruct((2, P_SIZE), F32)),
            in_specs=[vmem, vmem, pl.BlockSpec(memory_space=pltpu.SMEM)],
            out_specs=(vmem, vmem),
            scratch_shapes=[
                pltpu.VMEM((2, 8, P_SIZE), F32),
                pltpu.VMEM((36, 8, P_SIZE), F32),
                pltpu.VMEM((2, 3, P_SIZE, P_SIZE), F32),
                pltpu.VMEM((2, 27, P_SIZE, P_SIZE), F32),
                pltpu.VMEM((2, 9, P_SIZE, P_SIZE), F32),
                pltpu.VMEM((P_SIZE, P_SIZE), F32),
                pltpu.VMEM((2, 4, P_SIZE), F32),
                pltpu.VMEM((36, 4, P_SIZE), F32),
                pltpu.VMEM((3, 2, 1, P_SIZE), F32),
                pltpu.VMEM((3, 36, 1, P_SIZE), F32),
                pltpu.VMEM((3, 36, 8, P_SIZE), F32),
                pltpu.VMEM((1, 1, P_SIZE), F32),
                pltpu.VMEM((n_plane, 1, P_SIZE), F32),
                pltpu.VMEM((1, 1, P_SIZE), F32),
                pltpu.VMEM((n_length, 1, P_SIZE), F32),
                pltpu.SemaphoreType.DMA((5, N_OFF)),
                pltpu.SemaphoreType.DMA((5, N_OFF)),
                pltpu.SemaphoreType.DMA((2,)),
                pltpu.SemaphoreType.DMA((2,)),
            ],
            compiler_params=pltpu.CompilerParams(
                collective_id=0, has_side_effects=True, vmem_limit_bytes=32 * 1024 * 1024
            ),
            name="project",
        )(positions.reshape(3, 2, P_SIZE), velocity.reshape(3, 2, P_SIZE), counts.reshape(2))
        return moved.reshape(3, 1, 1, 2, P_SIZE), pressure.reshape(1, 1, 2, P_SIZE)

    return jax.shard_map(
        on_device,
        mesh=mesh,
        in_specs=(P(None, *AXES, None), P(None, *AXES, None), P(*AXES)),
        out_specs=(P(None, *AXES, None), P(*AXES, None)),
        check_vma=False,
    )
```

time: 860 us -> 57.9 us (0.07)
  blocking collectives: 506 us -> 0 us
  starting transfers between devices: 125 us -> 0 us
  matrix products: 72 us -> 0 us
  other arithmetic: 64.9 us -> 0 us
  Pallas kernels: 0 us -> 54.6 us
  waiting for transfers between devices: 54.6 us -> 0 us
  loops' own time: 19.8 us -> 0 us
    psum x5 -> x0, blocking collectives: 506 us -> none  [the longest x3 304 us: norm_sum(): return lax.psum(jnp.sum(residual * precond), ('gx', 'gy', 'gz'))]
    ppermute x48 -> x0, starting transfers between devices: 125 us -> none  [the longest x24 87.5 us: with_halo(): lax.ppermute(tail, axis, [(i, (i + 1) % count) for i in range(ends)])]
    dot_general x162 -> x0, matrix products: 72 us -> none  [the longest x81 30.4 us: laplace_fold(): jnp.einsum('tij,ctj->cti', weight, near_field, precision=lax.Precision.HI...]
    ppermute x48 -> x0, waiting for transfers between devices: 54.6 us -> none  [the longest x24 54.5 us: with_halo(): lax.ppermute(head, axis, [((i + 1) % count, i) for i in range(ends)])]
    pallas_call x0 -> x1, Pallas kernels: none -> 54.6 us  [on_device(): pl.pallas_call(functools.partial(kernel, sizes), out_shape=(jax.ShapeDtyp...]
    sub x163 -> x0, other arithmetic: 27 us -> none  [the longest x162 26.4 us: one_offset(): offset = own_positions[:, :, :, None] - near_positions[:, :, None, :]]
    another operation x6 -> x0, loops' own time: 19.8 us -> none  [slab_totals(): return lax.fori_loop(0, 27, one_offset, start_totals)]
    mul x217 -> x0, other arithmetic: 17.1 us -> none  [the longest x162 11.5 us: one_offset(): closeness * closeness * own_valid[:, :, None] * near_valid[:, None, :]]
  transfers between devices with their start and end apart: 48 -> 0, of which waited for: 17 -> 0; matrix products, arithmetic and copies ran while one was open for 0% -> 0% of each run, Pallas kernels for 0% -> 0%
where the time goes in v1:
time: 57.9 us; the launch traced here: 57.7 us
  Pallas kernels  54.6 us (94%)
  local copies, waits for them, and re-layouts  2.5 us (4%)
  between operations  0.66 us (1%)
    pallas_call x1, Pallas kernels, on_device(): pl.pallas_call(functools.partial(kernel, sizes), out_shape=(jax.ShapeDtyp...  54.6 us
    unnamed x8, local copies, waits for them, and re-layouts  2.5 us

profile of v1, /device:TPU:1, one launch (start us, length us, event | category | flops | bytes accessed | tf_op | source)
XLA Modules:
  0.0 57.7 jit_solution(18422948149572844676)
XLA Ops:
  0.6 0.0 copy-start
  0.6 0.0 copy-start.2
  0.6 0.7 %copy-done = f32[3,1,1,2,128]{4,3,2,1,0:T(2,128)S(1)} copy-done((f32[3,1,1,2,128]{4,3,2,1,0:T(2,128)S(1)}, f32[3,1,1,2,128]{4,3,2,1,0:T(2,128)}, u32[]{:S(2)}) %copy-start) | copy-done | bytes 3096
  1.3 0.0 copy-done.2
  1.3 0.0 copy-start.1
  1.3 0.7 %copy-done.1 = f32[3,1,1,2,128]{4,3,2,1,0:T(2,128)S(1)} copy-done((f32[3,1,1,2,128]{4,3,2,1,0:T(2,128)S(1)}, f32[3,1,1,2,128]{4,3,2,1,0:T(2,128)}, u32[]{:S(2)}) %copy-start.1) | copy-done | bytes 3096
  2.0 54.6 %project.1 = (f32[3,2,128]{2,1,0:T(2,128)S(1)}, f32[2,128]{1,0:T(2,128)S(1)}) custom-call(f32[3,2,128]{2,1,0:T(2,128)S(1)} %bitcast.8, f32[3,2,128]{2,1,0:T(2,128)S(1)} %bitcast.9, s32[2]{0:T(128)S(1)} %bitcast.11), custom_call_target="tpu_custom_call" | custom-call | tf_op jit(solution)/shard_map/project/pallas_call | solution.py:287
  56.6 0.6 %copy.8 = f32[3,1,1,2,128]{4,3,2,1,0:T(2,128)} copy(f32[3,1,1,2,128]{4,3,2,1,0:T(2,128)S(1)} %bitcast.7) | data formatting | bytes 6144
  57.2 0.6 copy.9
Async XLA Ops:
  0.6 0.7 %copy-start = (f32[3,1,1,2,128]{4,3,2,1,0:T(2,128)S(1)}, f32[3,1,1,2,128]{4,3,2,1,0:T(2,128)}, u32[]{:S(2)}) copy-start(f32[3,1,1,2,128]{4,3,2,1,0:T(2,128)} %param.3) | copy-start | bytes 9220
  0.6 0.7 %copy-start.2 = (s32[1,1,2]{2,1,0:T(1,128)S(1)}, s32[1,1,2]{2,1,0:T(1,128)}, u32[]{:S(2)}) copy-start(s32[1,1,2]{2,1,0:T(1,128)} %param.5) | copy-start | bytes 28
  1.3 0.7 %copy-start.1 = (f32[3,1,1,2,128]{4,3,2,1,0:T(2,128)S(1)}, f32[3,1,1,2,128]{4,3,2,1,0:T(2,128)}, u32[]{:S(2)}) copy-start(f32[3,1,1,2,128]{4,3,2,1,0:T(2,128)} %param.4) | copy-start | bytes 9220

commit v2 on v1

--- a/solution.py
+++ b/solution.py
@@ -9,6 +9,7 @@
 from jax.sharding import PartitionSpec as P
 
 P_SIZE = 128
+AWAY = 64.0
 DIAG_SHIFT = 0.05
 VISCOSITY = 0.5
 GRAVITY = 0.1
@@ -20,30 +21,33 @@
 OFFSETS = sorted((o for o in itertools.product((-1, 0, 1), repeat=3) if any(o)), key=lambda o: -sum(map(abs, o)))
 N_OFF = len(OFFSETS)
 OWN = 17
-GROUPS = (
-    ((0, 0),),
-    ((-1, 0), (1, 0), (0, -1), (0, 1)),
-    ((-1, -1), (-1, 1), (1, -1), (1, 1)),
-)
-
-
-def near_index(column, step_z):
-    return ((column[0] + 1) * 3 + column[1] + 1) * 3 + step_z
-
-
-def tile_index(column, own, step_z):
-    return ((column[0] + 1) * 3 + column[1] + 1) * 4 + own + step_z
-
-
-ALL_COLUMNS = tuple(c for g in GROUPS for c in g)
-
-
-def kernel(sizes, pos, vel, counts, vel_out, pres_out, x_own, x_halo, x_col, weights, sums, cols, p_own, p_halo, t_own,
+
+
+def pairs(own, hops):
+    found = []
+    for column in range(9):
+        for step in range(3):
+            across = abs(column // 3 - 1) + abs(column % 3 - 1) + (own + step in (0, 3))
+            if across in hops:
+                found.append((column * 4 + own + step, column * 3 + step))
+    return found
+
+
+ALL = (0, 1, 2, 3)
+
+
+def kernel(sizes, pos_in, vel_in, counts_in, vel_out, pres_out, pos, vel, counts, load, x_own, x_halo, x_col, weights, sums, cols, p_own, p_halo, t_own, t_sums,
            t_halo, levered, a_own, a_halo, b_own, b_halo, send, recv, a_sem, b_sem):
     me = [lax.axis_index(axis) for axis in AXES]
 
     def device(offset):
-        return tuple(lax.rem(m + (d + n), n) for m, d, n in zip(me, offset, sizes))
+        return tuple(lax.rem(m + (d + n), n) if d else m for m, d, n in zip(me, offset, sizes))
+
+    loads = [
+        pltpu.make_async_copy(a, b, load.at[i]) for i, (a, b) in enumerate(((pos_in, pos), (vel_in, vel), (counts_in, counts)))
+    ]
+    for item in loads:
+        item.start()
 
     plane = [(0, a, b) for a in range(sizes[1]) for b in range(sizes[2]) if a or b]
     length = [(a, 0, 0) for a in range(1, sizes[0])]
@@ -64,23 +68,24 @@
         else:
             pl.when(condition)(body)
 
-    x_halo[...] = jnp.zeros_like(x_halo)
-    p_halo[...] = jnp.zeros_like(p_halo)
-    t_halo[...] = jnp.zeros_like(t_halo)
+    x_halo[...] = jnp.full_like(x_halo, AWAY)
 
     barrier = pltpu.get_barrier_semaphore()
     greeted = OFFSETS + [(3, 0, 0), (-3, 0, 0)]
     for offset in greeted:
         pl.semaphore_signal(barrier, inc=1, device_id=device(offset), device_id_type=MESH)
 
+    p_halo[...] = jnp.zeros_like(p_halo)
+    t_halo[...] = jnp.zeros_like(t_halo)
+    for item in loads:
+        item.wait()
     lanes = lax.broadcasted_iota(jnp.int32, (1, P_SIZE), 1)
     valid = [(lanes < counts[t]).astype(F32) for t in range(2)]
     for t in range(2):
         for k in range(3):
-            x_own[t, k : k + 1] = pos[k, t : t + 1]
+            x_own[t, k : k + 1] = jnp.where(valid[t] > 0, pos[k, t : t + 1], AWAY)
             x_own[t, 3 + k : 4 + k] = vel[k, t : t + 1]
-        x_own[t, 6:7] = valid[t]
-        x_own[t, 7:8] = jnp.zeros((1, P_SIZE), F32)
+        x_own[t, 6:8] = jnp.zeros((2, P_SIZE), F32)
         x_halo[OWN + t] = x_own[t]
         for k in range(3):
             x_col[t, k] = jnp.broadcast_to(pos[k, t : t + 1], (P_SIZE, P_SIZE)).T
@@ -110,10 +115,10 @@
                         copy(phase, own, halo, (dx, dy, dz)).start()
             under(exists(dy, dz), body)
 
-    def arrive(phase, own, halo, columns):
+    def arrive(phase, own, halo, hops):
         for dy, dz in combos[::-1]:
-            steps = [-c[0] for c in columns if c[1] == -dy and (c[0] or dy or dz)]
-            if steps:
+            steps = [dx for dx in (-1, 0, 1) if abs(dx) + abs(dy) + abs(dz) == hops]
+            if steps and hops:
                 def body(dy=dy, dz=dz, steps=steps):
                     for dx in steps:
                         copy(phase, own, halo, (dx, dy, dz)).wait_recv()
@@ -138,59 +143,57 @@
         turned = cols[...].T
         return [[turned[16 * a + q : 16 * a + q + 1] for q in range(n)] for a in range(2)]
 
-    def apply(n, row_of, depth):
-        @pl.loop(0, P_SIZE // depth)
-        def _(block):
-            at = pl.ds(pl.multiple_of(block * depth, depth), depth)
-            for a in range(2):
-                totals = [jnp.zeros((depth, P_SIZE), F32)] * n
-                for column in ALL_COLUMNS:
-                    for dz in range(3):
-                        tile = tile_index(column, a, dz)
-                        w = weights[a, near_index(column, dz), at]
+    def apply(n, term, depth, exchange=None):
+        for hops in ((0,), (1,), (2,), (3,)) if exchange else (ALL,):
+            if exchange:
+                arrive(*exchange, hops[0])
+
+            @pl.loop(0, P_SIZE // depth)
+            def _(block, hops=hops):
+                at = pl.ds(pl.multiple_of(block * depth, depth), depth)
+                for a in range(2):
+                    if hops[0]:
+                        totals = [sums[a, q, at] for q in range(n)]
+                    else:
+                        totals = [jnp.zeros((depth, P_SIZE), F32)] * n
+                    for tile, place in pairs(a, hops):
+                        terms = term(a, at, tile, place)
                         for q in range(n):
-                            totals[q] = totals[q] + w * row_of(tile, q)
-                for q in range(n):
-                    sums[a, q, at] = totals[q]
+                            totals[q] = totals[q] + terms[q]
+                    for q in range(n):
+                        sums[a, q, at] = totals[q]
         return to_rows(n)
 
+    def offset(a, at, tile):
+        return [x_col[a, k, at] - x_halo[tile, k : k + 1] for k in range(3)]
+
+    def weigh(a, at, tile, place):
+        d = offset(a, at, tile)
+        near = jnp.maximum(1.0 - (d[0] * d[0] + d[1] * d[1] + d[2] * d[2]), 0.0)
+        w = near * near
+        weights[a, place, at] = w
+        return [w] + [w * x_halo[tile, 3 + k : 4 + k] for k in range(3)]
+
+    def lever_terms(a, at, tile, place):
+        w = weights[a, place, at]
+        return [w * d for d in offset(a, at, tile)]
+
+    def times(n, row_of):
+        def term(a, at, tile, place):
+            w = weights[a, place, at]
+            return [w * row_of(tile, q) for q in range(n)]
+        return term
+
     start(0, x_own, x_halo)
-    for number, columns in enumerate(GROUPS):
-        arrive(0, x_own, x_halo, columns)
-
-        @pl.loop(0, P_SIZE // 16)
-        def _(block, number=number, columns=columns):
-            at = pl.ds(pl.multiple_of(block * 16, 16), 16)
-            for a in range(2):
-                mine = [x_col[a, k, at] for k in range(3)]
-                if number:
-                    totals = [sums[a, q, at] for q in range(7)]
-                else:
-                    totals = [jnp.zeros((16, P_SIZE), F32)] * 7
-                for column in columns:
-                    for dz in range(3):
-                        tile = tile_index(column, a, dz)
-                        d = [mine[k] - x_halo[tile, k : k + 1] for k in range(3)]
-                        near = jnp.maximum(1.0 - (d[0] * d[0] + d[1] * d[1] + d[2] * d[2]), 0.0)
-                        w = near * near * x_halo[tile, 6:7]
-                        weights[a, near_index(column, dz), at] = w
-                        totals[0] = totals[0] + w
-                        for k in range(3):
-                            totals[1 + k] = totals[1 + k] + w * x_halo[tile, 3 + k : 4 + k]
-                            totals[4 + k] = totals[4 + k] + w * d[k]
-                for q in range(7):
-                    sums[a, q, at] = totals[q]
-
-    rows = to_rows(7)
+    rows = apply(4, weigh, 16, (0, x_own, x_halo))
     scale = 1.0 / P_SIZE
     centre = [s * 0.5 for s in (sizes[0], sizes[1], sizes[2] * 2)]
-    diagonal, lever, predicted, x = [], [], [], []
+    diagonal, predicted, x = [], [], []
     for a in range(2):
         row = rows[a][0] * valid[a]
         v = [vel[k, a : a + 1] for k in range(3)]
         x.append([pos[k, a : a + 1] - centre[k] for k in range(3)])
         diagonal.append(DIAG_SHIFT + row * scale)
-        lever.append([rows[a][4 + k] * valid[a] for k in range(3)])
         p = [valid[a] * (v[k] + VISCOSITY * scale * (rows[a][1 + k] - row * v[k]) - (GRAVITY if k == 2 else 0.0)) for k in range(3)]
         predicted.append(p)
         for k in range(3):
@@ -198,29 +201,27 @@
         p_own[a, 3:4] = p[0] * x[a][0] + p[1] * x[a][1] + p[2] * x[a][2]
     start(1, p_own, p_halo)
     p_halo[OWN : OWN + 2] = p_own[...]
-    arrive(1, p_own, p_halo, ALL_COLUMNS)
-    rows = apply(4, lambda tile, q: p_halo[tile, q : q + 1], 16)
-    basis, source = [[], [], [], []], []
+    rows = apply(3, lever_terms, 16)
+    lever = [[rows[a][k] * valid[a] for k in range(3)] for a in range(2)]
+    rows = apply(4, times(4, lambda tile, q: p_halo[tile, q : q + 1]), 64, (1, p_own, p_halo))
     for a in range(2):
         flux = x[a][0] * rows[a][0] + x[a][1] * rows[a][1] + x[a][2] * rows[a][2] - rows[a][3]
         dot = predicted[a][0] * lever[a][0] + predicted[a][1] * lever[a][1] + predicted[a][2] * lever[a][2]
-        source.append(valid[a] * (-(GRADIENT_GAIN * scale) * (dot - flux)))
-        basis[0].append(source[a] / diagonal[a])
-        t_own[0, a] = basis[0][a]
+        t_own[0, a] = valid[a] * (-(GRADIENT_GAIN * scale) * (dot - flux)) / diagonal[a]
     inverse = [scale * valid[a] / diagonal[a] for a in range(2)]
 
-    spread = []
-    for k in range(3):
-        start(2 + k, t_own.at[k], t_halo.at[k])
-        t_halo[k, OWN : OWN + 2] = t_own[k]
-        arrive(2 + k, t_own.at[k], t_halo.at[k], ALL_COLUMNS)
-        rows = apply(1, lambda tile, q, k=k: t_halo[k, tile], 32)
-        spread.append([rows[a][0] for a in range(2)])
+    @pl.loop(0, 3)
+    def _(k):
+        own, halo = t_own.at[k], t_halo.at[k]
+        start(2 + k, own, halo)
+        halo[OWN : OWN + 2] = own[...]
+        rows = apply(1, times(1, lambda tile, q: halo[tile]), 64, (2 + k, own, halo))
         for a in range(2):
-            basis[k + 1].append(spread[k][a] * inverse[a])
-            if k < 2:
-                t_own[k + 1, a] = basis[k + 1][a]
-
+            t_sums[k, a] = rows[a][0]
+            t_own[k + 1, a] = rows[a][0] * inverse[a]
+
+    basis = [[t_own[k, a] for a in range(2)] for k in range(4)]
+    spread = [[t_sums[k, a] for a in range(2)] for k in range(3)]
     packed = jnp.zeros((1, P_SIZE), F32)
     for q in range(6):
         i, j = q // 2, (q + 1) // 2
@@ -244,7 +245,7 @@
         local = x_halo[tile]
         for c in range(3):
             levered[c, tile] = (local[c : c + 1] - centre[c]) * jnp.concatenate([t_halo[k, tile] for k in range(3)] + [jnp.zeros((5, P_SIZE), F32)], axis=0)
-    rows = apply(9, lambda tile, q: levered[q // 3, tile, q % 3 : q % 3 + 1], 16)
+    rows = apply(9, times(9, lambda tile, q: levered[q // 3, tile, q % 3 : q % 3 + 1]), 16)
     moved = []
     for a in range(2):
         moved.append([
@@ -256,8 +257,11 @@
     share(length, b_own, b_halo, b_sem)
     sent(0, x_own, x_halo)
     sent(1, p_own, p_halo)
-    for k in range(3):
+
+    @pl.loop(0, 3)
+    def _(k):
         sent(2 + k, t_own.at[k], t_halo.at[k])
+
     pltpu.make_async_copy(a_halo, a_halo, a_sem.at[0]).wait()
     total = gathered(length, b_own, b_halo, b_sem)
 
@@ -287,9 +291,13 @@
         moved, pressure = pl.pallas_call(
             functools.partial(kernel, sizes),
             out_shape=(jax.ShapeDtypeStruct((3, 2, P_SIZE), F32), jax.ShapeDtypeStruct((2, P_SIZE), F32)),
-            in_specs=[vmem, vmem, pl.BlockSpec(memory_space=pltpu.SMEM)],
+            in_specs=[pl.BlockSpec(memory_space=pltpu.HBM)] * 3,
             out_specs=(vmem, vmem),
             scratch_shapes=[
+                pltpu.VMEM((3, 2, P_SIZE), F32),
+                pltpu.VMEM((3, 2, P_SIZE), F32),
+                pltpu.SMEM((2,), jnp.int32),
+                pltpu.SemaphoreType.DMA((3,)),
                 pltpu.VMEM((2, 8, P_SIZE), F32),
                 pltpu.VMEM((36, 8, P_SIZE), F32),
                 pltpu.VMEM((2, 3, P_SIZE, P_SIZE), F32),
@@ -298,6 +306,7 @@
                 pltpu.VMEM((P_SIZE, P_SIZE), F32),
                 pltpu.VMEM((2, 4, P_SIZE), F32),
                 pltpu.VMEM((36, 4, P_SIZE), F32),
+                pltpu.VMEM((4, 2, 1, P_SIZE), F32),
                 pltpu.VMEM((3, 2, 1, P_SIZE), F32),
                 pltpu.VMEM((3, 36, 1, P_SIZE), F32),
                 pltpu.VMEM((3, 36, 8, P_SIZE), F32),
@@ -311,7 +320,7 @@
                 pltpu.SemaphoreType.DMA((2,)),
             ],
             compiler_params=pltpu.CompilerParams(
-                collective_id=0, has_side_effects=True, vmem_limit_bytes=32 * 1024 * 1024
+                collective_id=0, has_side_effects=True, vmem_limit_bytes=55220 * 1024
             ),
             name="project",
         )(positions.reshape(3, 2, P_SIZE), velocity.reshape(3, 2, P_SIZE), counts.reshape(2))

time: 57.9 us -> 54.5 us (0.941)
  Pallas kernels: 54.6 us -> 51.9 us
  local copies, waits for them, and re-layouts: 2.5 us -> 1.79 us
    pallas_call x1, Pallas kernels: 54.6 us -> 51.9 us  [on_device(): pl.pallas_call(functools.partial(kernel, sizes), out_shape=(jax.ShapeDtyp...]
    unnamed x8 -> x4, local copies, waits for them, and re-layouts: 2.5 us -> 1.79 us
where the time goes in v2:
time: 54.5 us; the launch traced here: 54.4 us
  Pallas kernels  51.9 us (95%)
  local copies, waits for them, and re-layouts  1.79 us (3%)
  between operations  0.65 us (1%)
    pallas_call x1, Pallas kernels, on_device(): pl.pallas_call(functools.partial(kernel, sizes), out_shape=(jax.ShapeDtyp...  51.9 us
    unnamed x4, local copies, waits for them, and re-layouts  1.79 us

profile of v2, /device:TPU:1, one launch (start us, length us, event | category | flops | bytes accessed | tf_op | source)
XLA Modules:
  0.0 54.4 jit_solution(14352529220429119512)
XLA Ops:
  0.6 0.0 copy-start
  0.6 0.6 %copy-done = s32[1,1,2]{2,1,0:T(1,128)S(1)} copy-done((s32[1,1,2]{2,1,0:T(1,128)S(1)}, s32[1,1,2]{2,1,0:T(1,128)}, u32[]{:S(2)}) %copy-start) | copy-done | bytes 32
  1.3 51.9 %project.1 = (f32[3,2,128]{2,1,0:T(2,128)S(1)}, f32[2,128]{1,0:T(2,128)S(1)}) custom-call(f32[3,2,128]{2,1,0:T(2,128)} %bitcast.10, f32[3,2,128]{2,1,0:T(2,128)} %bitcast.11, s32[2]{0:T(128)S(1)} %bitcast.9), custom_call_target="tpu_custom_call" | custom-call | tf_op jit(solution)/shard_map/project/pallas_call | solution.py:291
  53.2 0.6 %copy.8 = f32[3,1,1,2,128]{4,3,2,1,0:T(2,128)} copy(f32[3,1,1,2,128]{4,3,2,1,0:T(2,128)S(1)} %bitcast.7) | data formatting | bytes 6144
  53.8 0.6 %copy.9 = f32[1,1,2,128]{3,2,1,0:T(2,128)} copy(f32[1,1,2,128]{3,2,1,0:T(2,128)S(1)} %bitcast.8) | data formatting | bytes 2048
Async XLA Ops:
  0.6 0.7 %copy-start = (s32[1,1,2]{2,1,0:T(1,128)S(1)}, s32[1,1,2]{2,1,0:T(1,128)}, u32[]{:S(2)}) copy-start(s32[1,1,2]{2,1,0:T(1,128)} %param.5) | copy-start | bytes 28

commit v3 on v2

--- a/solution.py
+++ b/solution.py
@@ -49,8 +49,11 @@
     for item in loads:
         item.start()
 
-    plane = [(0, a, b) for a in range(sizes[1]) for b in range(sizes[2]) if a or b]
-    length = [(a, 0, 0) for a in range(1, sizes[0])]
+    def far(offset):
+        return -sum(min(d, n - d) for d, n in zip(offset, sizes))
+
+    plane = sorted(((0, a, b) for a in range(sizes[1]) for b in range(sizes[2]) if a or b), key=far)
+    length = sorted(((a, 0, 0) for a in range(1, sizes[0])), key=far)
     inside = {
         (1, -1): me[1] > 0, (1, 1): me[1] < sizes[1] - 1,
         (2, -1): me[2] > 0, (2, 1): me[2] < sizes[2] - 1,
@@ -86,9 +89,6 @@
             x_own[t, k : k + 1] = jnp.where(valid[t] > 0, pos[k, t : t + 1], AWAY)
             x_own[t, 3 + k : 4 + k] = vel[k, t : t + 1]
         x_own[t, 6:8] = jnp.zeros((2, P_SIZE), F32)
-        x_halo[OWN + t] = x_own[t]
-        for k in range(3):
-            x_col[t, k] = jnp.broadcast_to(pos[k, t : t + 1], (P_SIZE, P_SIZE)).T
     pl.semaphore_wait(barrier, len(greeted))
 
     def copy(phase, own, halo, offset):
@@ -105,18 +105,18 @@
             source, target, send.at[phase, i], recv.at[phase, i], device_id=device(offset), device_id_type=MESH
         )
 
-    combos = sorted(itertools.product((-1, 0, 1), repeat=2), key=lambda c: -sum(map(abs, c)))
+    combos = sorted(itertools.product((-1, 0, 1), repeat=2), key=lambda c: sum(map(abs, c)))
 
     def start(phase, own, halo):
         for dy, dz in combos:
             def body(dy=dy, dz=dz):
-                for dx in (-1, 1, 0):
+                for dx in (0, -1, 1):
                     if dx or dy or dz:
                         copy(phase, own, halo, (dx, dy, dz)).start()
             under(exists(dy, dz), body)
 
     def arrive(phase, own, halo, hops):
-        for dy, dz in combos[::-1]:
+        for dy, dz in combos:
             steps = [dx for dx in (-1, 0, 1) if abs(dx) + abs(dy) + abs(dz) == hops]
             if steps and hops:
                 def body(dy=dy, dz=dz, steps=steps):
@@ -185,6 +185,10 @@
         return term
 
     start(0, x_own, x_halo)
+    for t in range(2):
+        x_halo[OWN + t] = x_own[t]
+        for k in range(3):
+            x_col[t, k] = jnp.broadcast_to(pos[k, t : t + 1], (P_SIZE, P_SIZE)).T
     rows = apply(4, weigh, 16, (0, x_own, x_halo))
     scale = 1.0 / P_SIZE
     centre = [s * 0.5 for s in (sizes[0], sizes[1], sizes[2] * 2)]
@@ -320,10 +324,10 @@
                 pltpu.SemaphoreType.DMA((2,)),
             ],
             compiler_params=pltpu.CompilerParams(
-                collective_id=0, has_side_effects=True, vmem_limit_bytes=55220 * 1024
+                collective_id=0, has_side_effects=True, vmem_limit_bytes=32 * 1024 * 1024
             ),
             name="project",
-        )(positions.reshape(3, 2, P_SIZE), velocity.reshape(3, 2, P_SIZE), counts.reshape(2))
+        )(*(pltpu.with_memory_space_constraint(v, pltpu.HBM) for v in (positions.reshape(3, 2, P_SIZE), velocity.reshape(3, 2, P_SIZE), counts.reshape(2))))
         return moved.reshape(3, 1, 1, 2, P_SIZE), pressure.reshape(1, 1, 2, P_SIZE)
 
     return jax.shard_map(

time: 54.5 us -> 52.9 us (0.971)
  Pallas kernels: 51.9 us -> 51 us
  local copies, waits for them, and re-layouts: 1.79 us -> 1.14 us
    pallas_call x1, Pallas kernels: 51.9 us -> 51 us  [on_device(): pl.pallas_call(functools.partial(kernel, sizes), out_shape=(jax.ShapeDtyp...]
    unnamed x4 -> x2, local copies, waits for them, and re-layouts: 1.79 us -> 1.14 us
where the time goes in v3:
time: 52.9 us; the launch traced here: 52.8 us
  Pallas kernels  51 us (96%)
  local copies, waits for them, and re-layouts  1.14 us (2%)
  between operations  0.64 us (1%)
    pallas_call x1, Pallas kernels, on_device(): pl.pallas_call(functools.partial(kernel, sizes), out_shape=(jax.ShapeDtyp...  51 us
    unnamed x2, local copies, waits for them, and re-layouts  1.14 us

profile of v3, /device:TPU:1, one launch (start us, length us, event | category | flops | bytes accessed | tf_op | source)
XLA Modules:
  0.0 52.8 jit_solution(12313328072129998078)
XLA Ops:
  0.6 51.0 %project.1 = (f32[3,2,128]{2,1,0:T(2,128)S(1)}, f32[2,128]{1,0:T(2,128)S(1)}) custom-call(f32[3,2,128]{2,1,0:T(2,128)} %bitcast.9, f32[3,2,128]{2,1,0:T(2,128)} %bitcast.10, s32[2]{0:T(128)} %bitcast.11), custom_call_target="tpu_custom_call" | custom-call | tf_op jit(solution)/shard_map/project/pallas_call | solution.py:295
  51.6 0.6 %copy.8 = f32[3,1,1,2,128]{4,3,2,1,0:T(2,128)} copy(f32[3,1,1,2,128]{4,3,2,1,0:T(2,128)S(1)} %bitcast.7) | data formatting | bytes 6144
  52.2 0.6 %copy.9 = f32[1,1,2,128]{3,2,1,0:T(2,128)} copy(f32[1,1,2,128]{3,2,1,0:T(2,128)S(1)} %bitcast.8) | data formatting | bytes 2048

commit v4 on v3

--- a/solution.py
+++ b/solution.py
@@ -328,6 +328,23 @@
             ),
             name="project",
         )(*(pltpu.with_memory_space_constraint(v, pltpu.HBM) for v in (positions.reshape(3, 2, P_SIZE), velocity.reshape(3, 2, P_SIZE), counts.reshape(2))))
+
+        def hand_over(moved, pressure, moved_out, pressure_out, sem):
+            first = pltpu.make_async_copy(moved, moved_out, sem.at[0])
+            second = pltpu.make_async_copy(pressure, pressure_out, sem.at[1])
+            first.start()
+            second.start()
+            first.wait()
+            second.wait()
+
+        moved, pressure = pl.pallas_call(
+            hand_over,
+            out_shape=(jax.ShapeDtypeStruct((3, 2, P_SIZE), F32), jax.ShapeDtypeStruct((2, P_SIZE), F32)),
+            in_specs=[vmem, vmem],
+            out_specs=(pl.BlockSpec(memory_space=pltpu.HBM),) * 2,
+            scratch_shapes=[pltpu.SemaphoreType.DMA((2,))],
+            name="hand_over",
+        )(*(pltpu.with_memory_space_constraint(v, pltpu.VMEM) for v in (moved, pressure)))
         return moved.reshape(3, 1, 1, 2, P_SIZE), pressure.reshape(1, 1, 2, P_SIZE)
 
     return jax.shard_map(

time: 52.9 us -> 52.4 us (level)
  local copies, waits for them, and re-layouts: 1.14 us -> 0 us
  Pallas kernels: 51 us -> 51.6 us
    unnamed x2 -> x0, local copies, waits for them, and re-layouts: 1.14 us -> none
    pallas_call x0 -> x1, Pallas kernels: none -> 0.6 us  [on_device(): pl.pallas_call(hand_over, out_shape=(jax.ShapeDtypeStruct((3, 2, P_SIZE),...]
where the time goes in v4:
time: 52.4 us; the launch traced here: 52.2 us
  Pallas kernels  51.6 us (98%)
  between operations  0.64 us (1%)
    pallas_call x1, Pallas kernels, on_device(): pl.pallas_call(functools.partial(kernel, sizes), out_shape=(jax.ShapeDtyp...  51 us

profile of v4, /device:TPU:1, one launch (start us, length us, event | category | flops | bytes accessed | tf_op | source)
XLA Modules:
  0.0 52.2 jit_solution(10307118752136397247)
XLA Ops:
  0.6 51.0 %project.1 = (f32[3,2,128]{2,1,0:T(2,128)S(1)}, f32[2,128]{1,0:T(2,128)S(1)}) custom-call(f32[3,2,128]{2,1,0:T(2,128)} %bitcast.7, f32[3,2,128]{2,1,0:T(2,128)} %bitcast.8, s32[2]{0:T(128)} %bitcast.9), custom_call_target="tpu_custom_call" | custom-call | tf_op jit(solution)/shard_map/project/pallas_call | solution.py:295
  51.6 0.6 %hand_over.1 = (f32[3,2,128]{2,1,0:T(2,128)}, f32[2,128]{1,0:T(2,128)}) custom-call(f32[3,2,128]{2,1,0:T(2,128)S(1)} %get-tuple-element.6.moved, f32[2,128]{1,0:T(2,128)S(1)} %get-tuple-element.7.pressure), custom_call_target="tpu_custom_call" | custom-call | tf_op jit(solution)/shard_map/hand_over/pallas_call | solution.py:340

commit v5 on v3

--- a/solution.py
+++ b/solution.py
@@ -205,6 +205,7 @@
         p_own[a, 3:4] = p[0] * x[a][0] + p[1] * x[a][1] + p[2] * x[a][2]
     start(1, p_own, p_halo)
     p_halo[OWN : OWN + 2] = p_own[...]
+    sent(0, x_own, x_halo)
     rows = apply(3, lever_terms, 16)
     lever = [[rows[a][k] * valid[a] for k in range(3)] for a in range(2)]
     rows = apply(4, times(4, lambda tile, q: p_halo[tile, q : q + 1]), 64, (1, p_own, p_halo))
@@ -257,10 +258,9 @@
             for c in range(3)
         ])
 
+    sent(1, p_own, p_halo)
     b_own[0] = gathered(plane, a_own, a_halo, a_sem)
     share(length, b_own, b_halo, b_sem)
-    sent(0, x_own, x_halo)
-    sent(1, p_own, p_halo)
 
     @pl.loop(0, 3)
     def _(k):

time: 52.9 us -> 52.9 us (level)
  no operation moved by 1% of the time
where the time goes in v5:
time: 52.9 us; the launch traced here: 52.8 us
  Pallas kernels  51 us (96%)
  local copies, waits for them, and re-layouts  1.14 us (2%)
  between operations  0.64 us (1%)
    pallas_call x1, Pallas kernels, on_device(): pl.pallas_call(functools.partial(kernel, sizes), out_shape=(jax.ShapeDtyp...  51 us
    unnamed x2, local copies, waits for them, and re-layouts  1.14 us

profile of v5, /device:TPU:1, one launch (start us, length us, event | category | flops | bytes accessed | tf_op | source)
XLA Modules:
  0.0 52.8 jit_solution(12543254706672995723)
XLA Ops:
  0.6 51.0 %project.1 = (f32[3,2,128]{2,1,0:T(2,128)S(1)}, f32[2,128]{1,0:T(2,128)S(1)}) custom-call(f32[3,2,128]{2,1,0:T(2,128)} %bitcast.9, f32[3,2,128]{2,1,0:T(2,128)} %bitcast.10, s32[2]{0:T(128)} %bitcast.11), custom_call_target="tpu_custom_call" | custom-call | tf_op jit(solution)/shard_map/project/pallas_call | solution.py:295
  51.6 0.6 %copy.8 = f32[3,1,1,2,128]{4,3,2,1,0:T(2,128)} copy(f32[3,1,1,2,128]{4,3,2,1,0:T(2,128)S(1)} %bitcast.7) | data formatting | bytes 6144
  52.2 0.6 %copy.9 = f32[1,1,2,128]{3,2,1,0:T(2,128)} copy(f32[1,1,2,128]{3,2,1,0:T(2,128)S(1)} %bitcast.8) | data formatting | bytes 2048
